TPU v7x, 256 devices: a whole 4x4x8 slice. The times are simulated.
256 devices in a mesh: crop: 2 (over core), row: 8 (over z), col: 16 (over y, x).
Axes of the slice: x: 4, y: 4, z: 8, core: 2. Of those that a mesh axis runs over, the one named last changes fastest.
Arguments:
- pair: float32 [2, 512, 512, 128], P('crop', 'row', 'col'), parts along dimension 0, may hold values from -6 to 6
- gain_input: float32 [128], replicated, may hold values from 0.1 to 1.9
- weights_in: float32 [128, 512], replicated, may hold values from -0.5 to 0.5
- gate_weights: float32 [128, 128], replicated, may hold values from -0.5 to 0.5
- weights_out: float32 [128, 128], replicated, may hold values from -0.5 to 0.5
- gain_product: float32 [128], replicated, may hold values from 0.1 to 1.9
- gain_transition: float32 [128], replicated, may hold values from 0.1 to 1.9
- transition_in: float32 [128, 1024], replicated, may hold values from -0.5 to 0.5
- transition_out: float32 [512, 128], replicated, may hold values from -0.25 to 0.25
- distogram_weights: float32 [128, 64], replicated, may hold values from -0.5 to 0.5
- distogram_bias: float32 [64], replicated, may hold values from -4 to 4
Outputs:
- logits: float32 [2, 512, 512, 64], P('crop', 'row', 'col'), parts along dimension 0
There are 2 independent parts, one for each index of `crop`. A program takes and returns all parts, laid end to end along the dimension named above; an argument that names none is the same for every part. Nothing has to cross between parts.
All inputs are finite; a program needn't handle non-finite values.
Results may differ from a plain program's by a relative error of at most 0.00007.
Values sent between devices are 32-bit elements; how exact they have to be, the bound alone decides.
A program may use at most 64 MiB of HBM per device.

v0:
```python
import functools

import jax
import jax.numpy as jnp
from jax import lax
from jax.experimental import pallas as pl
from jax.experimental.pallas import tpu as pltpu
from jax.sharding import PartitionSpec as P

MESH = pl.DeviceIdType.MESH
BF = jnp.bfloat16
F32 = jnp.float32
NZ = 8
NQ = 16

LR_XY, LR_Z, BASE, P_Z, P_XY, A1_XY, A2_Z, A2_XY, PHASES = 0, 4, 8, 9, 11, 13, 15, 17, 19


def split(values):
    high = values.astype(BF)
    return high, (values - high.astype(F32)).astype(BF)


def stack_right(values):
    high, low = split(values)
    return jnp.concatenate([high, low, high], axis=0)


def normalize(values):
    center = values - jnp.mean(values, axis=0, keepdims=True)
    spread = jnp.mean(center * center, axis=0, keepdims=True)
    return center * lax.rsqrt(spread + 1e-05)


def dot(left, right):
    return lax.dot_general(left, right, (((1,), (0,)), ((), ())), preferred_element_type=F32)


def dot_nt(left, right):
    return lax.dot_general(left, right, (((1,), (1,)), ((), ())), preferred_element_type=F32)


def sigmoid(values):
    return 1.0 / (1.0 + jnp.exp(-values))


def store_weights(target, row, weights, gain):
    depth = weights.shape[0]
    for part in range(depth // 128):
        turned = weights[part * 128 : (part + 1) * 128, :].T
        if gain is not None:
            turned = turned * gain
        high, low = split(turned)
        rows = pl.ds(row, turned.shape[0])
        at = part * 128
        target[rows, at : at + 128] = high
        target[rows, depth + at : depth + at + 128] = high
        target[rows, 2 * depth + at : 2 * depth + at + 128] = low


def kernel(
    pair,
    gain_in,
    w_in,
    w_gate,
    w_out,
    gain_prod,
    gain_trans,
    w_ti,
    w_to,
    w_dist,
    bias,
    out,
    win3,
    wgate3,
    wout3,
    wti3,
    wto3,
    wdist3,
    x3,
    sb1,
    rb1,
    sb2,
    rb2,
    base,
    xt,
    gate,
    r3,
    psb,
    prb,
    psx,
    prx,
    abuf,
    a1,
    a2m,
    a2f,
    send_sem,
    recv_sem,
):
    crop = lax.axis_index("crop")
    z = lax.axis_index("row")
    q = lax.axis_index("col")

    def to_plane(phase, source, target, count=NQ):
        def step(k, carry):
            peer = lax.rem(q + k, NQ)
            pltpu.make_async_remote_copy(
                src_ref=source(peer),
                dst_ref=target,
                send_sem=send_sem.at[phase],
                recv_sem=recv_sem.at[phase],
                device_id=(crop, z, peer),
                device_id_type=MESH,
            ).start()
            return carry

        lax.fori_loop(1, NQ, step, 0)
        pltpu.make_async_copy(source(q), target, recv_sem.at[phase]).start()

    def to_line(phase, source, target):
        def step(k, carry):
            peer = lax.rem(z + k, NZ)
            pltpu.make_async_remote_copy(
                src_ref=source(peer),
                dst_ref=target,
                send_sem=send_sem.at[phase],
                recv_sem=recv_sem.at[phase],
                device_id=(crop, peer, q),
                device_id_type=MESH,
            ).start()
            return carry

        lax.fori_loop(1, NZ, step, 0)
        pltpu.make_async_copy(source(z), target, recv_sem.at[phase]).start()

    def landed(phase, whole):
        pltpu.make_async_copy(whole, whole, recv_sem.at[phase]).wait()

    def sent(phase, most):
        pltpu.make_async_copy(most, most, send_sem.at[phase]).wait()

    barrier = pltpu.get_barrier_semaphore()

    def greet_plane(k, carry):
        pl.semaphore_signal(barrier, inc=1, device_id=(crop, z, lax.rem(q + k, NQ)), device_id_type=MESH)
        return carry

    def greet_line(k, carry):
        pl.semaphore_signal(barrier, inc=1, device_id=(crop, lax.rem(z + k, NZ), q), device_id_type=MESH)
        return carry

    lax.fori_loop(1, NQ, greet_plane, 0)
    lax.fori_loop(1, NZ, greet_line, 0)

    for block in range(4):
        store_weights(win3, block * 128, w_in[:, block * 128 : (block + 1) * 128], gain_in[...])

    def norm_chunk(h):
        def step(n, carry):
            blocks = []
            for u in range(4):
                rows = pair[:, h * 2 : h * 2 + 2, n * 4 + u, :, :]
                blocks.append(rows.reshape(128, 128).T)
            x3[h * 2 + n] = stack_right(normalize(jnp.concatenate(blocks, axis=1)))
            return carry

        lax.fori_loop(0, 2, step, 0)

    def project_chunk(side, h):
        first = 256 if side == 0 else 0

        def step(n, carry):
            both = dot(win3[first : first + 256, :], x3[h * 2 + n])
            value = sigmoid(both[128:, :]) * both[:128, :]
            for u in range(4):
                at = pl.multiple_of((n * 4 + u) * 8, 8)
                sb1[side * 2 + h, :, pl.ds(at, 8), :] = value[:, u * 128 : (u + 1) * 128].reshape(16, 8, 128)
            return carry

        lax.fori_loop(0, 2, step, 0)
        index = side * 2 + h
        to_plane(LR_XY + index, lambda peer: sb1.at[index, peer], rb1.at[index, q])

    lane = lax.broadcasted_iota(jnp.int32, (8, 128), 1)
    low_half = lane < 64
    even_block = lax.rem(lane, 64) < 32

    def relay_chunk(index):
        landed(LR_XY + index, rb1.at[index])

        def step(c, carry):
            for group in range(4):
                v = [rb1[index, group * 4 + u, pl.ds(c, 8, stride=8), :] for u in range(4)]
                s = [None] * 4
                for u in range(2):
                    s[u] = jnp.where(low_half, v[u], pltpu.roll(v[u + 2], 64, 1))
                    s[u + 2] = jnp.where(low_half, pltpu.roll(v[u], 64, 1), v[u + 2])
                for u in (0, 2):
                    first = jnp.where(even_block, s[u], pltpu.roll(s[u + 1], 32, 1))
                    second = jnp.where(even_block, pltpu.roll(s[u], 96, 1), s[u + 1])
                    lanes = slice(group * 128, (group + 1) * 128)
                    sb2[index, c, u * 8 : u * 8 + 8, lanes] = first
                    sb2[index, c, u * 8 + 8 : u * 8 + 16, lanes] = second
            return carry

        lax.fori_loop(0, 8, step, 0)
        to_line(LR_Z + index, lambda peer: sb2.at[index, peer], rb2.at[index, z])

    norm_chunk(0)
    project_chunk_ready = pl.semaphore_wait(barrier, NQ - 1 + NZ - 1)
    del project_chunk_ready
    project_chunk(0, 0)
    norm_chunk(1)
    project_chunk(0, 1)
    project_chunk(1, 0)
    relay_chunk(0)
    project_chunk(1, 1)
    relay_chunk(1)

    def pair_source(peer):
        return pair.at[peer // 8, :, lax.rem(peer, 8)]

    to_plane(BASE, pair_source, base.at[q])
    relay_chunk(2)
    relay_chunk(3)

    store_weights(wgate3, 0, w_gate[...], gain_in[...])
    store_weights(wout3, 0, w_out[...], gain_prod[...])
    for block in range(8):
        store_weights(wti3, block * 128, w_ti[:, block * 128 : (block + 1) * 128], gain_trans[...])
    store_weights(wto3, 0, w_to[...], None)
    store_weights(wdist3, 0, w_dist[...], None)

    landed(BASE, base)

    def base_step(hb, carry):
        blocks = [base[g * 4 : g * 4 + 4, hb].reshape(128, 128).T for g in range(4)]
        value = jnp.concatenate(blocks, axis=1)
        xt[hb] = value
        gate[hb] = sigmoid(dot(wgate3[...], stack_right(normalize(value))))
        return carry

    lax.fori_loop(0, 4, base_step, 0)

    for h in range(2):
        landed(LR_Z + h, rb2.at[h])

        def right_step(n, carry):
            zz, a = n // 2, lax.rem(n, 2)
            high, low = split(rb2[h, zz, pl.ds(pl.multiple_of(a * 16, 16), 16), :])
            rows = pl.ds(pl.multiple_of(zz * 64 + a * 32 + h * 16, 16), 16)
            r3[rows, 0:512] = high
            r3[rows, 512:1024] = low
            r3[rows, 1024:1536] = high
            return carry

        lax.fori_loop(0, 16, right_step, 0)

    for h in range(2):
        landed(LR_Z + 2 + h, rb2.at[2 + h])
        high, low = split(rb2[2 + h].reshape(256, 512))
        l3 = jnp.concatenate([high, high, low], axis=1)
        for jt in range(4):
            product = dot_nt(l3, r3[jt * 128 : (jt + 1) * 128, :])
            for zz in range(8):
                at = zz * 128 + jt * 32
                psb[h, at : at + 32, :] = product[zz * 32 : (zz + 1) * 32, :]
        to_line(
            P_Z + h,
            lambda peer: psb.at[h, pl.ds(pl.multiple_of(peer * 128, 128), 128), :],
            prb.at[h, pl.ds(pl.multiple_of(z * 128, 128), 128), :],
        )

    def product_relay(h):
        landed(P_Z + h, prb.at[h])

        def step(row, carry):
            m = (row // 16) * 8 + lax.rem(row, 8)
            b = lax.rem(row // 8, 2)
            for jt in range(4):
                psx[h, m, b * 4 + jt] = prb[h, pl.ds(jt * 32 + row, 8, stride=128), :]
            return carry

        lax.fori_loop(0, 32, step, 0)
        to_plane(P_XY + h, lambda peer: psx.at[h, peer], prx.at[h, q])

    def transition(h):
        landed(P_XY + h, prx.at[h])
        logits = []
        for b in range(2):
            hb = h * 2 + b
            product = jnp.concatenate([prx[h, :, b * 4 + jt].reshape(128, 128) for jt in range(4)], axis=1)
            updated = xt[hb] + gate[hb] * dot(wout3[...], stack_right(normalize(product)))
            right = stack_right(normalize(updated))
            total = updated
            for part in range(2):
                at = part * 256
                up_gate = dot(wti3[at : at + 256, :], right)
                up = dot(wti3[512 + at : 768 + at, :], right)
                high, low = split(up_gate * sigmoid(up_gate) * up)
                total = total + dot(wto3[:, at : at + 256], high)
                total = total + dot(wto3[:, 512 + at : 768 + at], low)
                total = total + dot(wto3[:, 1024 + at : 1280 + at], high)
            logits.append(dot(wdist3[...], stack_right(total)))
        stacked = jnp.concatenate(logits, axis=0)
        for jt in range(4):
            abuf[h, jt * 128 : (jt + 1) * 128, :] = stacked[:, jt * 128 : (jt + 1) * 128].T
        to_line(
            A2_Z + h,
            lambda peer: abuf.at[h, pl.ds(pl.multiple_of(peer * 64, 64), 64), :],
            a2m.at[h, z],
        )
        to_plane(
            A1_XY + h,
            lambda peer: abuf.at[h, pl.ds(pl.multiple_of(peer * 32, 32), 32), :],
            a1.at[h, q],
        )

    own = lax.rem(q, 2) == q // 8

    def mirror_relay(h):
        landed(A2_Z + h, a2m.at[h])
        target = a2f.at[h, pl.ds(pl.multiple_of(lax.rem(q, 8) * 64, 64), 64), :]

        def step(k, carry):
            zz = lax.rem(z + k, NZ)
            peer = 2 * zz + q // 8

            @pl.when(peer != q)
            def _():
                pltpu.make_async_remote_copy(
                    src_ref=a2m.at[h, zz],
                    dst_ref=target,
                    send_sem=send_sem.at[A2_XY + h],
                    recv_sem=recv_sem.at[A2_XY + h],
                    device_id=(crop, z, peer),
                    device_id_type=MESH,
                ).start()

            @pl.when(peer == q)
            def _():
                pltpu.make_async_copy(a2m.at[h, zz], target, recv_sem.at[A2_XY + h]).start()

            return carry

        lax.fori_loop(0, NZ, step, 0)

    product_relay(0)
    transition(0)
    product_relay(1)
    mirror_relay(0)
    transition(1)
    mirror_relay(1)

    for h in range(2):
        landed(A1_XY + h, a1.at[h])
        landed(A2_XY + h, a2f.at[h])

    both_bias = jnp.concatenate([bias[...], bias[...]], axis=1)

    def final_step(m, carry):
        first = (m // 8) * 32 + lax.rem(m, 8)
        for h in range(2):
            for h2 in range(2):
                mine = [a1[h, m, h2 * 16 + b2 * 8 : h2 * 16 + b2 * 8 + 8, :] + both_bias for b2 in range(2)]
                for b in range(2):
                    i = first + h * 16 + b * 8
                    other = a2f[h2, pl.ds(i, 8, stride=64), :]
                    turned = pltpu.roll(other, 64, 1)
                    for b2 in range(2):
                        value = mine[b2] + (other if b == b2 else turned)
                        if b:
                            value = pltpu.roll(value, 64, 1)
                        out[i, h2 * 16 + b2 * 8 : h2 * 16 + b2 * 8 + 8, :] = value[:, :64]
        return carry

    lax.fori_loop(0, NQ, final_step, 0)

    for index in range(4):
        sent(LR_XY + index, sb1.at[index, pl.ds(0, NQ - 1)])
        sent(LR_Z + index, sb2.at[index, pl.ds(0, NZ - 1)])
    sent(BASE, base.at[pl.ds(0, NQ - 1)])
    for h in range(2):
        sent(P_Z + h, psb.at[h, pl.ds(0, 128 * (NZ - 1)), :])
        sent(P_XY + h, psx.at[h, pl.ds(0, NQ - 1)])
        sent(A1_XY + h, abuf.at[h, pl.ds(0, 32 * (NQ - 1)), :])
        sent(A2_Z + h, abuf.at[h, pl.ds(0, 64 * (NZ - 1)), :])

        @pl.when(own)
        def _():
            sent(A2_XY + h, a2m.at[h, pl.ds(0, NZ - 1)])

        @pl.when(jnp.logical_not(own))
        def _():
            sent(A2_XY + h, a2m.at[h])


def shards(pair, gain_in, w_in, w_gate, w_out, gain_prod, gain_trans, w_ti, w_to, w_dist, bias):
    vmem = pl.BlockSpec(memory_space=pltpu.VMEM)
    result = pl.pallas_call(
        kernel,
        out_shape=jax.ShapeDtypeStruct((64, 32, 64), F32),
        in_specs=[vmem] * 11,
        out_specs=vmem,
        scratch_shapes=[
            pltpu.VMEM((512, 384), BF),
            pltpu.VMEM((128, 384), BF),
            pltpu.VMEM((128, 384), BF),
            pltpu.VMEM((1024, 384), BF),
            pltpu.VMEM((128, 1536), BF),
            pltpu.VMEM((64, 384), BF),
            pltpu.VMEM((4, 384, 512), BF),
            pltpu.VMEM((4, 16, 64, 128), F32),
            pltpu.VMEM((4, 16, 64, 128), F32),
            pltpu.VMEM((4, 8, 32, 512), F32),
            pltpu.VMEM((4, 8, 32, 512), F32),
            pltpu.VMEM((16, 4, 32, 128), F32),
            pltpu.VMEM((4, 128, 512), F32),
            pltpu.VMEM((4, 128, 512), F32),
            pltpu.VMEM((512, 1536), BF),
            pltpu.VMEM((2, 1024, 128), F32),
            pltpu.VMEM((2, 1024, 128), F32),
            pltpu.VMEM((2, 16, 8, 8, 128), F32),
            pltpu.VMEM((2, 16, 8, 8, 128), F32),
            pltpu.VMEM((2, 512, 128), F32),
            pltpu.VMEM((2, 16, 32, 128), F32),
            pltpu.VMEM((2, 8, 64, 128), F32),
            pltpu.VMEM((2, 512, 128), F32),
            pltpu.SemaphoreType.DMA((PHASES,)),
            pltpu.SemaphoreType.DMA((PHASES,)),
        ],
        compiler_params=pltpu.CompilerParams(
            collective_id=0, has_side_effects=True, vmem_limit_bytes=56 * 1024 * 1024
        ),
        name="triangle",
    )(
        pair.reshape(2, 4, 8, 32, 128),
        gain_in.reshape(1, 128),
        w_in,
        w_gate,
        w_out,
        gain_prod.reshape(1, 128),
        gain_trans.reshape(1, 128),
        w_ti,
        w_to,
        w_dist,
        bias.reshape(1, 64),
    )
    return result.reshape(1, 64, 32, 64)


def solution(mesh):
    return jax.shard_map(
        shards,
        mesh=mesh,
        in_specs=(P("crop", "row", "col", None), P(), P(), P(), P(), P(), P(), P(), P(), P(), P()),
        out_specs=P("crop", "row", "col", None),
        check_vma=False,
    )
```

profile of v0, /device:TPU:24, one launch (start us, length us, event | category | flops | bytes accessed | tf_op | source)
XLA Modules:
  0.0 131.0 jit_solution(13406932049738669474)
XLA Ops:
  0.0 1.5 %copy.12.w_dist = f32[128,64]{1,0:T(8,128)} copy(f32[128,64]{0,1:T(8,128)} %param.20) | data formatting | bytes 65536 | tf_op args[9]
  1.5 127.2 %triangle.1 = f32[64,32,64]{2,1,0:T(8,128)} custom-call(f32[2,4,8,32,128]{4,3,2,1,0:T(8,128)} %bitcast.7, f32[1,128]{1,0:T(1,128)} %bitcast.8, f32[128,512]{1,0:T(8,128)} %w_in.1, f32[128,128]{1,0:T(8,128)} %w_gate.1, f32[128,128]{1,0:T(8,128)} %w_out.1, f32[1,128]{1,0:T(1,128)} %bitcast.9, f32[1,128]{1,0:T(1,128)} %bitcast.10, f32[128,1024]{1,0:T(8,128)} %w_ti.1, ...), custom_call_target="tpu_custom_call" | custom-call | tf_op jit(solution)/shard_map/triangle/pallas_call | solution.py:400
  128.7 2.3 %copy.14 = f32[1,64,32,64]{3,2,1,0:T(8,128)} copy(f32[1,64,32,64]{3,2,1,0:T(8,128)} %bitcast.6) | data formatting | bytes 1048576
where the time goes:
time: 131 us
  Pallas kernels  127 us (97%)
  local copies, waits for them, and re-layouts  3.75 us (3%)
    pallas_call x1, Pallas kernels, shards(): pl.pallas_call(kernel, out_shape=jax.ShapeDtypeStruct((64, 32, 64), F32),...  127 us
    unnamed x2, local copies, waits for them, and re-layouts  3.75 us

commit v1 on v0

v1 whole, which is shorter than its diff:
```python
import jax
import jax.numpy as jnp
from jax import lax
from jax.experimental import pallas as pl
from jax.experimental.pallas import tpu as pltpu
from jax.sharding import PartitionSpec as P

MESH = pl.DeviceIdType.MESH
BF = jnp.bfloat16
F32 = jnp.float32
NZ = 8
NQ = 16
ND = NZ * NQ

LR, BASE, PROD, A1, A2Z, A2Q, PHASES = 0, 4, 5, 7, 11, 15, 19


def split(values):
    high = values.astype(BF)
    return high, (values - high.astype(F32)).astype(BF)


def stack_right(values):
    high, low = split(values)
    return jnp.concatenate([high, low, high], axis=0)


def normalize(values):
    center = values - jnp.mean(values, axis=0, keepdims=True)
    spread = jnp.mean(center * center, axis=0, keepdims=True)
    return center * lax.rsqrt(spread + 1e-05)


def dot(left, right):
    return lax.dot_general(left, right, (((1,), (0,)), ((), ())), preferred_element_type=F32)


def dot_nt(left, right):
    return lax.dot_general(left, right, (((1,), (1,)), ((), ())), preferred_element_type=F32)


def sigmoid(values):
    return 1.0 / (1.0 + jnp.exp(-values))


def store_weights(target, row, weights, gain, turn=True):
    depth = weights.shape[0] if turn else 128
    for part in range(depth // 128):
        turned = weights[part * 128 : (part + 1) * 128, :].T if turn else weights
        if gain is not None:
            turned = turned * gain
        high, low = split(turned)
        rows = pl.ds(row, turned.shape[0])
        at = part * 128
        target[rows, at : at + 128] = high
        target[rows, depth + at : depth + at + 128] = high
        target[rows, 2 * depth + at : 2 * depth + at + 128] = low


def kernel(
    pair,
    gain_in,
    w_in,
    w_gate,
    w_out,
    gain_prod,
    gain_trans,
    w_ti,
    w_to,
    w_dist,
    bias,
    out,
    win3,
    wgate3,
    wout3,
    wti3,
    wto3,
    wdist3,
    x3,
    sb,
    rb,
    base,
    xt,
    gate,
    right_high,
    right_low,
    left_high,
    left_low,
    psb,
    prb,
    abuf,
    a1,
    a2m,
    a2f,
    send_sem,
    recv_sem,
    line_sem,
):
    crop = lax.axis_index("crop")
    z = lax.axis_index("row")
    q = lax.axis_index("col")
    me = z * NQ + q

    def remote(phase, source, target, zz, qq):
        pltpu.make_async_remote_copy(
            src_ref=source,
            dst_ref=target,
            send_sem=send_sem.at[phase],
            recv_sem=recv_sem.at[phase],
            device_id=(crop, zz, qq),
            device_id_type=MESH,
        ).start()

    def local(phase, source, target):
        pltpu.make_async_copy(source, target, recv_sem.at[phase]).start()

    def to_all(phase, source, target, beside=None):
        with jax.named_scope("issue_%d" % phase):
            for k in range(1, NZ):
                zz = lax.rem(z + k, NZ)
                remote(phase, source(zz * NQ + q), target, zz, q)

            def step(k, carry):
                qq = lax.rem(q + k, NQ)
                for kz in range(NZ):
                    zz = lax.rem(z + kz, NZ)
                    remote(phase, source(zz * NQ + qq), target, zz, qq)
                if beside is not None:
                    beside(qq)
                return carry

            lax.fori_loop(1, NQ, step, 0)
            local(phase, source(me), target)

    def to_plane(phase, source, target):
        def step(k, carry):
            qq = lax.rem(q + k, NQ)
            remote(phase, source(qq), target, z, qq)
            return carry

        lax.fori_loop(1, NQ, step, 0)
        local(phase, source(q), target)

    def to_line(phase, source, target):
        for k in range(1, NZ):
            zz = lax.rem(z + k, NZ)
            remote(phase, source(zz), target, zz, q)
        local(phase, source(z), target)

    def landed(phase, whole):
        with jax.named_scope("wait_%d" % phase):
            pltpu.make_async_copy(whole, whole, recv_sem.at[phase]).wait()

    def sent(phase, most):
        pltpu.make_async_copy(most, most, send_sem.at[phase]).wait()

    barrier = pltpu.get_barrier_semaphore()

    def greet_plane(k, carry):
        pl.semaphore_signal(barrier, inc=1, device_id=(crop, z, lax.rem(q + k, NQ)), device_id_type=MESH)
        return carry

    lax.fori_loop(1, NQ, greet_plane, 0)
    for k in range(1, NZ):
        pl.semaphore_signal(barrier, inc=1, device_id=(crop, lax.rem(z + k, NZ), q), device_id_type=MESH)

    for block in (2, 3, 0, 1):
        store_weights(win3, block * 128, w_in[:, block * 128 : (block + 1) * 128], gain_in[...])

    def norm_chunk(h):
        def step(n, carry):
            blocks = []
            for u in range(4):
                rows = pair[:, h * 2 : h * 2 + 2, n * 4 + u, :, :]
                blocks.append(rows.reshape(128, 128).T)
            x3[h * 2 + n] = stack_right(normalize(jnp.concatenate(blocks, axis=1)))
            return carry

        with jax.named_scope("norm"):
            lax.fori_loop(0, 2, step, 0)

    def project_chunk(side, h):
        first = 256 if side == 0 else 0
        index = side * 2 + h

        def step(n, carry):
            both = dot(win3[first : first + 256, :], x3[h * 2 + n])
            value = sigmoid(both[128:, :]) * both[:128, :]
            for u in range(4):
                sb[index, pl.ds(n * 4 + u, 128, stride=8), :] = value[:, u * 128 : (u + 1) * 128]
            return carry

        with jax.named_scope("project"):
            lax.fori_loop(0, 2, step, 0)

    def send_chunk(index, beside=None):
        to_all(
            LR + index,
            lambda p: sb.at[index, pl.ds(pl.multiple_of(p * 8, 8), 8), :],
            rb.at[index, me],
            beside,
        )

    def pair_source(peer):
        return pair.at[peer // 8, :, lax.rem(peer, 8)]

    norm_chunk(0)
    with jax.named_scope("wait_barrier"):
        pl.semaphore_wait(barrier, NQ - 1 + NZ - 1)
    for k in range(1, NZ):
        pl.semaphore_signal(line_sem, inc=1, device_id=(crop, lax.rem(z + k, NZ), q), device_id_type=MESH)
    project_chunk(0, 0)
    with jax.named_scope("wait_line"):
        pl.semaphore_wait(line_sem, NZ - 1)
    send_chunk(0)
    norm_chunk(1)
    project_chunk(0, 1)
    send_chunk(1)
    project_chunk(1, 0)
    send_chunk(2, lambda qq: remote(BASE, pair_source(qq), base.at[q], z, qq))
    local(BASE, pair_source(q), base.at[q])
    project_chunk(1, 1)
    send_chunk(3)

    with jax.named_scope("weights"):
        store_weights(wgate3, 0, w_gate[...], gain_in[...])
        store_weights(wout3, 0, w_out[...], gain_prod[...])
        for block in range(8):
            store_weights(wti3, block * 128, w_ti[:, block * 128 : (block + 1) * 128], gain_trans[...])
        store_weights(wto3, 0, w_to[...], None)
        store_weights(wdist3, 0, w_dist[...], None, turn=False)

    lane = lax.broadcasted_iota(jnp.int32, (8, 128), 1)
    low_half = lane < 64
    even_block = lax.rem(lane, 64) < 32

    def assemble(index, high_ref, low_ref, first):
        landed(LR + index, rb.at[index])

        def step(zz, carry):
            for group in range(4):
                v = [rb[index, zz * NQ + group * 4 + u] for u in range(4)]
                s = [None] * 4
                for u in range(2):
                    s[u] = jnp.where(low_half, v[u], pltpu.roll(v[u + 2], 64, 1))
                    s[u + 2] = jnp.where(low_half, pltpu.roll(v[u], 64, 1), v[u + 2])
                for a in range(2):
                    even, odd = s[2 * a], s[2 * a + 1]
                    both = jnp.concatenate(
                        [
                            jnp.where(even_block, even, pltpu.roll(odd, 32, 1)),
                            jnp.where(even_block, pltpu.roll(even, 96, 1), odd),
                        ],
                        axis=0,
                    )
                    high, low = split(both)
                    rows = pl.ds(pl.multiple_of(first + zz * 32 + a * 16, 16), 16)
                    high_ref[rows, group * 128 : (group + 1) * 128] = high
                    low_ref[rows, group * 128 : (group + 1) * 128] = low
            return carry

        with jax.named_scope("assemble"):
            lax.fori_loop(0, NZ, step, 0)

    assemble(0, right_high, right_low, 0)
    assemble(1, right_high, right_low, 256)

    def multiply(h):
        assemble(2 + h, left_high, left_low, 0)
        with jax.named_scope("product"):
            for half in range(2):
                rows = slice(half * 256, half * 256 + 256)
                product = (
                    dot_nt(left_high[...], right_high[rows, :])
                    + dot_nt(left_high[...], right_low[rows, :])
                    + dot_nt(left_low[...], right_high[rows, :])
                )
                for zz in range(NZ):
                    for a in range(2):
                        for b in range(2):
                            row = zz * 32 + a * 16 + b * 8
                            for u in range(2):
                                start = (zz * 16 + a * 8) * 8 + b * 4 + half * 2 + u
                                psb[h, pl.ds(start, 8, stride=8), :] = product[row : row + 8, u * 128 : (u + 1) * 128]
        to_all(
            PROD + h,
            lambda p: psb.at[h, pl.ds(pl.multiple_of(p * 8, 8), 8), :],
            prb.at[h, pl.ds(pl.multiple_of(me * 8, 8), 8), :],
        )

    multiply(0)
    landed(BASE, base)

    def base_step(hb, carry):
        blocks = []
        for jt in range(4):
            some = base[(jt % 2) * 8 : (jt % 2) * 8 + 8, hb, (jt // 2) * 16 : (jt // 2) * 16 + 16, :]
            blocks.append(some.reshape(128, 128).T)
        value = jnp.concatenate(blocks, axis=1)
        xt[hb] = value
        gate[hb] = sigmoid(dot(wgate3[...], stack_right(normalize(value))))
        return carry

    with jax.named_scope("base_gate"):
        lax.fori_loop(0, 4, base_step, 0)
    multiply(1)

    target = pl.ds(pl.multiple_of(lax.rem(q, 8) * 32, 32), 32)

    def transition(h, b):
        hb = h * 2 + b
        with jax.named_scope("transition"):
            product = jnp.concatenate(
                [prb[h, pl.ds(b * 4 + jt, 128, stride=8), :] for jt in range(4)], axis=1
            )
            updated = xt[hb] + gate[hb] * dot(wout3[...], stack_right(normalize(product)))
            right = stack_right(normalize(updated))
            total = updated
            for part in range(2):
                at = part * 256
                up_gate = dot(wti3[at : at + 256, :], right)
                up = dot(wti3[512 + at : 768 + at, :], right)
                high, low = split(up_gate * sigmoid(up_gate) * up)
                total = total + dot(wto3[:, at : at + 256], high)
                total = total + dot(wto3[:, 512 + at : 768 + at], low)
                total = total + dot(wto3[:, 1024 + at : 1280 + at], high)
            logits = dot(wdist3[...], stack_right(total))
            stacked = jnp.concatenate([logits[:, :256], logits[:, 256:]], axis=0)
            for u in range(2):
                abuf[hb, u * 128 : (u + 1) * 128, :] = stacked[:, u * 128 : (u + 1) * 128].T
        if hb < 3:
            to_line(
                A2Z + hb,
                lambda zz: abuf.at[hb, pl.ds(pl.multiple_of(zz * 32, 32), 32), :],
                a2m.at[hb, z],
            )
        else:
            mirror(hb, lambda zz: abuf.at[hb, pl.ds(pl.multiple_of(zz * 32, 32), 32), :], True)
        to_plane(
            A1 + hb,
            lambda qq: abuf.at[hb, pl.ds(pl.multiple_of(qq * 16, 16), 16), :],
            a1.at[hb, q],
        )

    own = lax.rem(q, 2) == q // 8
    own_direct = 2 * z + q // 8 == q

    def mirror(hb, source, direct):
        def step(k, carry):
            zz = lax.rem(z + k, NZ)
            plane = zz if direct else z
            peer = 2 * (z if direct else zz) + q // 8
            here = jnp.logical_and(plane == z, peer == q)

            @pl.when(jnp.logical_not(here))
            def _():
                remote(A2Q + hb, source(zz), a2f.at[hb, target, :], plane, peer)

            @pl.when(here)
            def _():
                local(A2Q + hb, source(zz), a2f.at[hb, target, :])

            return carry

        lax.fori_loop(0, NZ, step, 0)

    def mirror_relay(hb):
        landed(A2Z + hb, a2m.at[hb])
        mirror(hb, lambda zz: a2m.at[hb, zz], False)

    landed(PROD, prb.at[0])
    transition(0, 0)
    transition(0, 1)
    landed(PROD + 1, prb.at[1])
    transition(1, 0)
    mirror_relay(0)
    mirror_relay(1)
    transition(1, 1)
    mirror_relay(2)

    for hb in range(4):
        landed(A1 + hb, a1.at[hb])
        landed(A2Q + hb, a2f.at[hb])

    both_bias = jnp.concatenate([bias[...], bias[...]], axis=1)

    def final_step(m, carry):
        a, t = m // 8, lax.rem(m, 8)
        for b in range(2):
            for bj in range(2):
                mine = [a1[h * 2 + b, m, bj * 8 : bj * 8 + 8, :] + both_bias for h in range(2)]
                other = [a2f[hj * 2 + bj, pl.ds(a * 16 + b * 8 + t, 8, stride=32), :] for hj in range(2)]
                values = (
                    (mine[0] + other[0], pltpu.roll(mine[0], 64, 1) + other[1]),
                    (mine[1] + pltpu.roll(other[0], 64, 1), pltpu.roll(mine[1] + other[1], 64, 1)),
                )
                for h in range(2):
                    i = a * 32 + h * 16 + b * 8 + t
                    for hj in range(2):
                        j = hj * 16 + bj * 8
                        out[i, j : j + 8, :] = values[h][hj][:, :64]
        return carry

    with jax.named_scope("final"):
        lax.fori_loop(0, NQ, final_step, 0)

    for index in range(4):
        sent(LR + index, rb.at[index, pl.ds(0, ND - 1)])
    sent(BASE, base.at[pl.ds(0, NQ - 1)])
    for h in range(2):
        sent(PROD + h, psb.at[h, pl.ds(0, 8 * (ND - 1)), :])
    for hb in range(4):
        sent(A1 + hb, a1.at[hb, pl.ds(0, NQ - 1)])
        if hb < 3:
            sent(A2Z + hb, a2m.at[hb, pl.ds(0, NZ - 1)])
        kept = own if hb < 3 else own_direct

        @pl.when(kept)
        def _():
            sent(A2Q + hb, a2m.at[hb, pl.ds(0, NZ - 1)])

        @pl.when(jnp.logical_not(kept))
        def _():
            sent(A2Q + hb, a2m.at[hb])


def shards(pair, gain_in, w_in, w_gate, w_out, gain_prod, gain_trans, w_ti, w_to, w_dist, bias):
    vmem = pl.BlockSpec(memory_space=pltpu.VMEM)
    result = pl.pallas_call(
        kernel,
        out_shape=jax.ShapeDtypeStruct((64, 32, 64), F32),
        in_specs=[vmem] * 11,
        out_specs=vmem,
        scratch_shapes=[
            pltpu.VMEM((512, 384), BF),
            pltpu.VMEM((128, 384), BF),
            pltpu.VMEM((128, 384), BF),
            pltpu.VMEM((1024, 384), BF),
            pltpu.VMEM((128, 1536), BF),
            pltpu.VMEM((64, 384), BF),
            pltpu.VMEM((4, 384, 512), BF),
            pltpu.VMEM((4, ND * 8, 128), F32),
            pltpu.VMEM((4, ND, 8, 128), F32),
            pltpu.VMEM((16, 4, 32, 128), F32),
            pltpu.VMEM((4, 128, 512), F32),
            pltpu.VMEM((4, 128, 512), F32),
            pltpu.VMEM((512, 512), BF),
            pltpu.VMEM((512, 512), BF),
            pltpu.VMEM((256, 512), BF),
            pltpu.VMEM((256, 512), BF),
            pltpu.VMEM((2, ND * 8, 128), F32),
            pltpu.VMEM((2, ND * 8, 128), F32),
            pltpu.VMEM((4, 256, 128), F32),
            pltpu.VMEM((4, 16, 16, 128), F32),
            pltpu.VMEM((4, 8, 32, 128), F32),
            pltpu.VMEM((4, 256, 128), F32),
            pltpu.SemaphoreType.DMA((PHASES,)),
            pltpu.SemaphoreType.DMA((PHASES,)),
            pltpu.SemaphoreType.REGULAR,
        ],
        compiler_params=pltpu.CompilerParams(
            collective_id=0, has_side_effects=True, vmem_limit_bytes=56 * 1024 * 1024
        ),
        name="triangle",
    )(
        pair.reshape(2, 4, 8, 32, 128),
        gain_in.reshape(1, 128),
        w_in,
        w_gate,
        w_out,
        gain_prod.reshape(1, 128),
        gain_trans.reshape(1, 128),
        w_ti,
        w_to,
        w_dist.T,
        bias.reshape(1, 64),
    )
    return result.reshape(1, 64, 32, 64)


def solution(mesh):
    return jax.shard_map(
        shards,
        mesh=mesh,
        in_specs=(P("crop", "row", "col", None), P(), P(), P(), P(), P(), P(), P(), P(), P(), P()),
        out_specs=P("crop", "row", "col", None),
        check_vma=False,
    )
```

time: 131 us -> 108 us (0.82); the launches traced: 131 us -> 107 us
  Pallas kernels: 127 us -> 104 us
  local copies, waits for them, and re-layouts: 3.75 us -> 2.26 us
    pallas_call x1, Pallas kernels: 127 us -> 104 us  [shards(): pl.pallas_call(kernel, out_shape=jax.ShapeDtypeStruct((64, 32, 64), F32),...]
    unnamed x2 -> x1, local copies, waits for them, and re-layouts: 3.75 us -> 2.26 us
where the time goes in v1:
time: 108 us; the launch traced here: 107 us
  Pallas kernels  104 us (96%)
  local copies, waits for them, and re-layouts  2.26 us (2%)
    pallas_call x1, Pallas kernels, shards(): pl.pallas_call(kernel, out_shape=jax.ShapeDtypeStruct((64, 32, 64), F32),...  104 us
    unnamed x1, local copies, waits for them, and re-layouts  2.26 us

profile of v1, /device:TPU:24, one launch (start us, length us, event | category | flops | bytes accessed | tf_op | source)
XLA Modules:
  0.0 106.6 jit_solution(9730144879439450660)
XLA Ops:
  0.0 104.3 %triangle.1 = f32[64,32,64]{2,1,0:T(8,128)} custom-call(f32[2,4,8,32,128]{4,3,2,1,0:T(8,128)} %bitcast.8, f32[1,128]{1,0:T(1,128)} %bitcast.10, f32[128,512]{1,0:T(8,128)} %w_in.1, f32[128,128]{1,0:T(8,128)} %w_gate.1, f32[128,128]{1,0:T(8,128)} %w_out.1, f32[1,128]{1,0:T(1,128)} %bitcast.11, f32[1,128]{1,0:T(1,128)} %bitcast.12, f32[128,1024]{1,0:T(8,128)} %w_ti.1, ...), custom_call_target="tpu_custom_call" | custom-call | tf_op jit(solution)/shard_map/triangle/pallas_call | solution.py:429
  104.3 2.3 %copy.13 = f32[1,64,32,64]{3,2,1,0:T(8,128)} copy(f32[1,64,32,64]{3,2,1,0:T(8,128)} %bitcast.7) | data formatting | bytes 1048576

commit v2 on v1

--- a/solution.py
+++ b/solution.py
@@ -12,7 +12,8 @@
 NQ = 16
 ND = NZ * NQ
 
-LR, BASE, PROD, A1, A2Z, A2Q, PHASES = 0, 4, 5, 7, 11, 15, 19
+LR, BASE, PROD, A1, A2, PHASES = 0, 4, 5, 7, 11, 15
+AROUND = (1, 7, 2, 6, 3, 5, 4)
 
 
 def split(values):
@@ -58,18 +59,25 @@
 
 
 def kernel(
+    pair_hbm,
+    gain_in,
+    w_in_hbm,
+    w_gate_hbm,
+    w_out_hbm,
+    gain_prod,
+    gain_trans,
+    w_ti_hbm,
+    w_to_hbm,
+    w_dist_hbm,
+    a1,
+    a2f,
     pair,
-    gain_in,
     w_in,
     w_gate,
     w_out,
-    gain_prod,
-    gain_trans,
     w_ti,
     w_to,
     w_dist,
-    bias,
-    out,
     win3,
     wgate3,
     wout3,
@@ -89,12 +97,10 @@
     psb,
     prb,
     abuf,
-    a1,
-    a2m,
-    a2f,
     send_sem,
     recv_sem,
     line_sem,
+    load_sem,
 ):
     crop = lax.axis_index("crop")
     z = lax.axis_index("row")
@@ -116,13 +122,13 @@
 
     def to_all(phase, source, target, beside=None):
         with jax.named_scope("issue_%d" % phase):
-            for k in range(1, NZ):
+            for k in AROUND:
                 zz = lax.rem(z + k, NZ)
                 remote(phase, source(zz * NQ + q), target, zz, q)
 
             def step(k, carry):
                 qq = lax.rem(q + k, NQ)
-                for kz in range(NZ):
+                for kz in AROUND + (0,):
                     zz = lax.rem(z + kz, NZ)
                     remote(phase, source(zz * NQ + qq), target, zz, qq)
                 if beside is not None:
@@ -141,12 +147,6 @@
         lax.fori_loop(1, NQ, step, 0)
         local(phase, source(q), target)
 
-    def to_line(phase, source, target):
-        for k in range(1, NZ):
-            zz = lax.rem(z + k, NZ)
-            remote(phase, source(zz), target, zz, q)
-        local(phase, source(z), target)
-
     def landed(phase, whole):
         with jax.named_scope("wait_%d" % phase):
             pltpu.make_async_copy(whole, whole, recv_sem.at[phase]).wait()
@@ -164,8 +164,31 @@
     for k in range(1, NZ):
         pl.semaphore_signal(barrier, inc=1, device_id=(crop, lax.rem(z + k, NZ), q), device_id_type=MESH)
 
-    for block in (2, 3, 0, 1):
-        store_weights(win3, block * 128, w_in[:, block * 128 : (block + 1) * 128], gain_in[...])
+    loads = [
+        pltpu.make_async_copy(source, target, load_sem.at[n])
+        for n, (source, target) in enumerate(
+            (
+                (w_in_hbm, w_in),
+                (pair_hbm, pair),
+                (w_gate_hbm, w_gate),
+                (w_out_hbm, w_out),
+                (w_ti_hbm, w_ti),
+                (w_to_hbm, w_to),
+                (w_dist_hbm, w_dist),
+            )
+        )
+    ]
+    for load in loads:
+        load.start()
+
+    def input_weights(blocks):
+        for block in blocks:
+            store_weights(win3, block * 128, w_in[:, block * 128 : (block + 1) * 128], gain_in[...])
+
+    with jax.named_scope("load_first"):
+        loads[0].wait()
+        input_weights((2, 3))
+        loads[1].wait()
 
     def norm_chunk(h):
         def step(n, carry):
@@ -202,20 +225,44 @@
         )
 
     def pair_source(peer):
-        return pair.at[peer // 8, :, lax.rem(peer, 8)]
+        return pair.at[lax.rem(peer, 2), :, peer // 2]
+
+    def send_first():
+        source = lambda p: sb.at[0, pl.ds(pl.multiple_of(p * 8, 8), 8), :]
+        target = rb.at[0, me]
+        for k in AROUND:
+            zz = lax.rem(z + k, NZ)
+            with jax.named_scope("wait_line"):
+                pl.semaphore_wait(line_sem.at[k], 1)
+
+            def step(kq, carry):
+                qq = lax.rem(q + kq, NQ)
+                remote(LR, source(zz * NQ + qq), target, zz, qq)
+                return carry
+
+            lax.fori_loop(0, NQ, step, 0)
+
+        def plane_step(kq, carry):
+            qq = lax.rem(q + kq, NQ)
+            remote(LR, source(z * NQ + qq), target, z, qq)
+            return carry
+
+        lax.fori_loop(1, NQ, plane_step, 0)
+        local(LR, source(me), target)
 
     norm_chunk(0)
+    project_chunk(0, 0)
     with jax.named_scope("wait_barrier"):
         pl.semaphore_wait(barrier, NQ - 1 + NZ - 1)
     for k in range(1, NZ):
-        pl.semaphore_signal(line_sem, inc=1, device_id=(crop, lax.rem(z + k, NZ), q), device_id_type=MESH)
-    project_chunk(0, 0)
-    with jax.named_scope("wait_line"):
-        pl.semaphore_wait(line_sem, NZ - 1)
-    send_chunk(0)
+        pl.semaphore_signal(
+            line_sem.at[NZ - k], inc=1, device_id=(crop, lax.rem(z + k, NZ), q), device_id_type=MESH
+        )
+    send_first()
     norm_chunk(1)
     project_chunk(0, 1)
     send_chunk(1)
+    input_weights((0, 1))
     project_chunk(1, 0)
     send_chunk(2, lambda qq: remote(BASE, pair_source(qq), base.at[q], z, qq))
     local(BASE, pair_source(q), base.at[q])
@@ -223,6 +270,8 @@
     send_chunk(3)
 
     with jax.named_scope("weights"):
+        for load in loads[2:]:
+            load.wait()
         store_weights(wgate3, 0, w_gate[...], gain_in[...])
         store_weights(wout3, 0, w_out[...], gain_prod[...])
         for block in range(8):
@@ -280,8 +329,8 @@
                         for b in range(2):
                             row = zz * 32 + a * 16 + b * 8
                             for u in range(2):
-                                start = (zz * 16 + a * 8) * 8 + b * 4 + half * 2 + u
-                                psb[h, pl.ds(start, 8, stride=8), :] = product[row : row + 8, u * 128 : (u + 1) * 128]
+                                start = (zz * 16 + a) * 8 + b * 4 + half * 2 + u
+                                psb[h, pl.ds(start, 8, stride=16), :] = product[row : row + 8, u * 128 : (u + 1) * 128]
         to_all(
             PROD + h,
             lambda p: psb.at[h, pl.ds(pl.multiple_of(p * 8, 8), 8), :],
@@ -304,8 +353,6 @@
     with jax.named_scope("base_gate"):
         lax.fori_loop(0, 4, base_step, 0)
     multiply(1)
-
-    target = pl.ds(pl.multiple_of(lax.rem(q, 8) * 32, 32), 32)
 
     def transition(h, b):
         hb = h * 2 + b
@@ -328,81 +375,40 @@
             stacked = jnp.concatenate([logits[:, :256], logits[:, 256:]], axis=0)
             for u in range(2):
                 abuf[hb, u * 128 : (u + 1) * 128, :] = stacked[:, u * 128 : (u + 1) * 128].T
-        if hb < 3:
-            to_line(
-                A2Z + hb,
-                lambda zz: abuf.at[hb, pl.ds(pl.multiple_of(zz * 32, 32), 32), :],
-                a2m.at[hb, z],
-            )
-        else:
-            mirror(hb, lambda zz: abuf.at[hb, pl.ds(pl.multiple_of(zz * 32, 32), 32), :], True)
+        mirror(hb)
         to_plane(
             A1 + hb,
             lambda qq: abuf.at[hb, pl.ds(pl.multiple_of(qq * 16, 16), 16), :],
-            a1.at[hb, q],
+            a1.at[hb, q // 2, lax.rem(q, 2)],
         )
 
-    own = lax.rem(q, 2) == q // 8
-    own_direct = 2 * z + q // 8 == q
-
-    def mirror(hb, source, direct):
-        def step(k, carry):
+    twin = 2 * z + lax.rem(q, 2)
+
+    def mirror(hb):
+        target = a2f.at[hb, q // 2]
+        for k in AROUND:
             zz = lax.rem(z + k, NZ)
-            plane = zz if direct else z
-            peer = 2 * (z if direct else zz) + q // 8
-            here = jnp.logical_and(plane == z, peer == q)
-
-            @pl.when(jnp.logical_not(here))
-            def _():
-                remote(A2Q + hb, source(zz), a2f.at[hb, target, :], plane, peer)
-
-            @pl.when(here)
-            def _():
-                local(A2Q + hb, source(zz), a2f.at[hb, target, :])
-
-            return carry
-
-        lax.fori_loop(0, NZ, step, 0)
-
-    def mirror_relay(hb):
-        landed(A2Z + hb, a2m.at[hb])
-        mirror(hb, lambda zz: a2m.at[hb, zz], False)
+            remote(A2 + hb, abuf.at[hb, pl.ds(pl.multiple_of(zz * 32, 32), 32), :], target, zz, twin)
+        source = abuf.at[hb, pl.ds(pl.multiple_of(z * 32, 32), 32), :]
+
+        @pl.when(twin != q)
+        def _():
+            remote(A2 + hb, source, target, z, twin)
+
+        @pl.when(twin == q)
+        def _():
+            local(A2 + hb, source, target)
 
     landed(PROD, prb.at[0])
     transition(0, 0)
     transition(0, 1)
     landed(PROD + 1, prb.at[1])
     transition(1, 0)
-    mirror_relay(0)
-    mirror_relay(1)
     transition(1, 1)
-    mirror_relay(2)
 
     for hb in range(4):
         landed(A1 + hb, a1.at[hb])
-        landed(A2Q + hb, a2f.at[hb])
-
-    both_bias = jnp.concatenate([bias[...], bias[...]], axis=1)
-
-    def final_step(m, carry):
-        a, t = m // 8, lax.rem(m, 8)
-        for b in range(2):
-            for bj in range(2):
-                mine = [a1[h * 2 + b, m, bj * 8 : bj * 8 + 8, :] + both_bias for h in range(2)]
-                other = [a2f[hj * 2 + bj, pl.ds(a * 16 + b * 8 + t, 8, stride=32), :] for hj in range(2)]
-                values = (
-                    (mine[0] + other[0], pltpu.roll(mine[0], 64, 1) + other[1]),
-                    (mine[1] + pltpu.roll(other[0], 64, 1), pltpu.roll(mine[1] + other[1], 64, 1)),
-                )
-                for h in range(2):
-                    i = a * 32 + h * 16 + b * 8 + t
-                    for hj in range(2):
-                        j = hj * 16 + bj * 8
-                        out[i, j : j + 8, :] = values[h][hj][:, :64]
-        return carry
-
-    with jax.named_scope("final"):
-        lax.fori_loop(0, NQ, final_step, 0)
+        landed(A2 + hb, a2f.at[hb])
 
     for index in range(4):
         sent(LR + index, rb.at[index, pl.ds(0, ND - 1)])
@@ -410,28 +416,53 @@
     for h in range(2):
         sent(PROD + h, psb.at[h, pl.ds(0, 8 * (ND - 1)), :])
     for hb in range(4):
-        sent(A1 + hb, a1.at[hb, pl.ds(0, NQ - 1)])
-        if hb < 3:
-            sent(A2Z + hb, a2m.at[hb, pl.ds(0, NZ - 1)])
-        kept = own if hb < 3 else own_direct
-
-        @pl.when(kept)
+        sent(A1 + hb, abuf.at[hb, pl.ds(0, 16 * (NQ - 1)), :])
+
+        @pl.when(twin == q)
         def _():
-            sent(A2Q + hb, a2m.at[hb, pl.ds(0, NZ - 1)])
-
-        @pl.when(jnp.logical_not(kept))
+            sent(A2 + hb, abuf.at[hb, pl.ds(0, 32 * (NZ - 1)), :])
+
+        @pl.when(twin != q)
         def _():
-            sent(A2Q + hb, a2m.at[hb])
+            sent(A2 + hb, abuf.at[hb])
+
+
+def add_mirrored(a1, a2f, bias, out):
+    both_bias = jnp.concatenate([bias[...], bias[...]], axis=1)
+    for b in range(2):
+        for bj in range(2):
+            for t in range(8):
+                mine = [a1[h * 2 + b, t, 0, bj * 8 : bj * 8 + 8, :] + both_bias for h in range(2)]
+                other = [a2f[hj * 2 + bj, :, b * 8 + t, :] for hj in range(2)]
+                values = (
+                    (mine[0] + other[0], pltpu.roll(mine[0], 64, 1) + other[1]),
+                    (mine[1] + pltpu.roll(other[0], 64, 1), pltpu.roll(mine[1] + other[1], 64, 1)),
+                )
+                for h in range(2):
+                    for hj in range(2):
+                        j = hj * 16 + bj * 8
+                        out[h * 16 + b * 8 + t, j : j + 8, :] = values[h][hj][:, :64]
 
 
 def shards(pair, gain_in, w_in, w_gate, w_out, gain_prod, gain_trans, w_ti, w_to, w_dist, bias):
     vmem = pl.BlockSpec(memory_space=pltpu.VMEM)
-    result = pl.pallas_call(
+    hbm = pl.BlockSpec(memory_space=pl.ANY)
+    own, mirrored = pl.pallas_call(
         kernel,
-        out_shape=jax.ShapeDtypeStruct((64, 32, 64), F32),
-        in_specs=[vmem] * 11,
-        out_specs=vmem,
+        out_shape=(
+            jax.ShapeDtypeStruct((4, 8, 2, 16, 128), F32),
+            jax.ShapeDtypeStruct((4, 8, 32, 128), F32),
+        ),
+        in_specs=[hbm, vmem, hbm, hbm, hbm, vmem, vmem, hbm, hbm, hbm],
+        out_specs=(hbm, hbm),
         scratch_shapes=[
+            pltpu.VMEM((2, 4, 8, 32, 128), F32),
+            pltpu.VMEM((128, 512), F32),
+            pltpu.VMEM((128, 128), F32),
+            pltpu.VMEM((128, 128), F32),
+            pltpu.VMEM((128, 1024), F32),
+            pltpu.VMEM((512, 128), F32),
+            pltpu.VMEM((64, 128), F32),
             pltpu.VMEM((512, 384), BF),
             pltpu.VMEM((128, 384), BF),
             pltpu.VMEM((128, 384), BF),
@@ -451,12 +482,10 @@
             pltpu.VMEM((2, ND * 8, 128), F32),
             pltpu.VMEM((2, ND * 8, 128), F32),
             pltpu.VMEM((4, 256, 128), F32),
-            pltpu.VMEM((4, 16, 16, 128), F32),
-            pltpu.VMEM((4, 8, 32, 128), F32),
-            pltpu.VMEM((4, 256, 128), F32),
             pltpu.SemaphoreType.DMA((PHASES,)),
             pltpu.SemaphoreType.DMA((PHASES,)),
-            pltpu.SemaphoreType.REGULAR,
+            pltpu.SemaphoreType.REGULAR((NZ,)),
+            pltpu.SemaphoreType.DMA((7,)),
         ],
         compiler_params=pltpu.CompilerParams(
             collective_id=0, has_side_effects=True, vmem_limit_bytes=56 * 1024 * 1024
@@ -473,8 +502,19 @@
         w_ti,
         w_to,
         w_dist.T,
-        bias.reshape(1, 64),
     )
+    result = pl.pallas_call(
+        add_mirrored,
+        grid=(2,),
+        out_shape=jax.ShapeDtypeStruct((64, 32, 64), F32),
+        in_specs=[
+            pl.BlockSpec((4, 8, 1, 16, 128), lambda a: (0, 0, a, 0, 0)),
+            pl.BlockSpec((4, 8, 16, 128), lambda a: (0, 0, a, 0)),
+            pl.BlockSpec((1, 64), lambda a: (0, 0)),
+        ],
+        out_specs=pl.BlockSpec((32, 32, 64), lambda a: (a, 0, 0)),
+        name="add_mirrored",
+    )(own, mirrored, bias.reshape(1, 64))
     return result.reshape(1, 64, 32, 64)
 
 

time: 108 us -> 101 us (0.935)
  Pallas kernels: 104 us -> 100 us
  local copies, waits for them, and re-layouts: 2.26 us -> 0 us
    pallas_call x1 -> x2, Pallas kernels: 104 us -> 100 us  [the longest x1 98.1 us: shards(): pl.pallas_call(kernel, out_shape=(jax.ShapeDtypeStruct((4, 8, 2, 16, 128)...]
    unnamed x1 -> x0, local copies, waits for them, and re-layouts: 2.26 us -> none
where the time goes in v2:
time: 101 us; the launch traced here: 100 us
  Pallas kernels  100 us (99%)
    pallas_call x1, Pallas kernels, shards(): pl.pallas_call(kernel, out_shape=(jax.ShapeDtypeStruct((4, 8, 2, 16, 128)...  98.1 us
    pallas_call x1, Pallas kernels, shards(): pl.pallas_call(add_mirrored, grid=(2,), out_shape=jax.ShapeDtypeStruct((6...  2.33 us

profile of v2, /device:TPU:24, one launch (start us, length us, event | category | flops | bytes accessed | tf_op | source)
XLA Modules:
  0.0 100.5 jit_solution(5917687080385274671)
XLA Ops:
  0.0 98.1 %triangle.1 = (f32[4,8,2,16,128]{4,3,2,1,0:T(8,128)}, f32[4,8,32,128]{3,2,1,0:T(8,128)}) custom-call(f32[2,4,8,32,128]{4,3,2,1,0:T(8,128)} %bitcast.7, f32[1,128]{1,0:T(1,128)} %bitcast.9, f32[128,512]{1,0:T(8,128)} %w_in_hbm.1, f32[128,128]{1,0:T(8,128)} %w_gate_hbm.1, f32[128,128]{1,0:T(8,128)} %w_out_hbm.1, f32[1,128]{1,0:T(1,128)} %bitcast.10, ...), custom_call_target="tpu_custom_call" | custom-call | tf_op jit(solution)/shard_map/triangle/pallas_call | solution.py:450
  98.2 2.3 %add_mirrored.1 = f32[64,32,64]{2,1,0:T(8,128)} custom-call(f32[4,8,2,16,128]{4,3,2,1,0:T(8,128)} %get-tuple-element.7.a1, f32[4,8,32,128]{3,2,1,0:T(8,128)} %get-tuple-element.8.a2f, f32[1,64]{1,0:T(1,128)} %bitcast.12), custom_call_target="tpu_custom_call" | custom-call | tf_op jit(solution)/shard_map/add_mirrored/pallas_call | solution.py:506

commit v3 on v2

--- a/solution.py
+++ b/solution.py
@@ -60,12 +60,12 @@
 
 def kernel(
     pair_hbm,
-    gain_in,
+    gain_in_hbm,
     w_in_hbm,
     w_gate_hbm,
     w_out_hbm,
-    gain_prod,
-    gain_trans,
+    gain_prod_hbm,
+    gain_trans_hbm,
     w_ti_hbm,
     w_to_hbm,
     w_dist_hbm,
@@ -78,6 +78,9 @@
     w_ti,
     w_to,
     w_dist,
+    gain_in,
+    gain_prod,
+    gain_trans,
     win3,
     wgate3,
     wout3,
@@ -154,32 +157,37 @@
     def sent(phase, most):
         pltpu.make_async_copy(most, most, send_sem.at[phase]).wait()
 
-    barrier = pltpu.get_barrier_semaphore()
-
-    def greet_plane(k, carry):
-        pl.semaphore_signal(barrier, inc=1, device_id=(crop, z, lax.rem(q + k, NQ)), device_id_type=MESH)
-        return carry
-
-    lax.fori_loop(1, NQ, greet_plane, 0)
-    for k in range(1, NZ):
-        pl.semaphore_signal(barrier, inc=1, device_id=(crop, lax.rem(z + k, NZ), q), device_id_type=MESH)
-
     loads = [
         pltpu.make_async_copy(source, target, load_sem.at[n])
         for n, (source, target) in enumerate(
             (
-                (w_in_hbm, w_in),
-                (pair_hbm, pair),
+                (gain_in_hbm, gain_in),
+                (w_in_hbm.at[:, 256:512], w_in.at[:, 256:512]),
+                (pair_hbm.at[:, 0:2], pair.at[:, 0:2]),
+                (pair_hbm.at[:, 2:4], pair.at[:, 2:4]),
+                (w_in_hbm.at[:, 0:256], w_in.at[:, 0:256]),
                 (w_gate_hbm, w_gate),
                 (w_out_hbm, w_out),
+                (gain_prod_hbm, gain_prod),
+                (gain_trans_hbm, gain_trans),
                 (w_ti_hbm, w_ti),
                 (w_to_hbm, w_to),
                 (w_dist_hbm, w_dist),
             )
         )
     ]
-    for load in loads:
+    for load in loads[:3]:
         load.start()
+
+    barrier = pltpu.get_barrier_semaphore()
+
+    def greet_plane(k, carry):
+        pl.semaphore_signal(barrier, inc=1, device_id=(crop, z, lax.rem(q + k, NQ)), device_id_type=MESH)
+        return carry
+
+    lax.fori_loop(1, NQ, greet_plane, 0)
+    for k in range(1, NZ):
+        pl.semaphore_signal(barrier, inc=1, device_id=(crop, lax.rem(z + k, NZ), q), device_id_type=MESH)
 
     def input_weights(blocks):
         for block in blocks:
@@ -187,8 +195,11 @@
 
     with jax.named_scope("load_first"):
         loads[0].wait()
+        loads[1].wait()
         input_weights((2, 3))
-        loads[1].wait()
+        loads[2].wait()
+    for load in loads[3:]:
+        load.start()
 
     def norm_chunk(h):
         def step(n, carry):
@@ -259,9 +270,11 @@
             line_sem.at[NZ - k], inc=1, device_id=(crop, lax.rem(z + k, NZ), q), device_id_type=MESH
         )
     send_first()
+    loads[3].wait()
     norm_chunk(1)
     project_chunk(0, 1)
     send_chunk(1)
+    loads[4].wait()
     input_weights((0, 1))
     project_chunk(1, 0)
     send_chunk(2, lambda qq: remote(BASE, pair_source(qq), base.at[q], z, qq))
@@ -270,7 +283,7 @@
     send_chunk(3)
 
     with jax.named_scope("weights"):
-        for load in loads[2:]:
+        for load in loads[5:]:
             load.wait()
         store_weights(wgate3, 0, w_gate[...], gain_in[...])
         store_weights(wout3, 0, w_out[...], gain_prod[...])
@@ -445,7 +458,6 @@
 
 
 def shards(pair, gain_in, w_in, w_gate, w_out, gain_prod, gain_trans, w_ti, w_to, w_dist, bias):
-    vmem = pl.BlockSpec(memory_space=pltpu.VMEM)
     hbm = pl.BlockSpec(memory_space=pl.ANY)
     own, mirrored = pl.pallas_call(
         kernel,
@@ -453,7 +465,7 @@
             jax.ShapeDtypeStruct((4, 8, 2, 16, 128), F32),
             jax.ShapeDtypeStruct((4, 8, 32, 128), F32),
         ),
-        in_specs=[hbm, vmem, hbm, hbm, hbm, vmem, vmem, hbm, hbm, hbm],
+        in_specs=[hbm] * 10,
         out_specs=(hbm, hbm),
         scratch_shapes=[
             pltpu.VMEM((2, 4, 8, 32, 128), F32),
@@ -463,6 +475,9 @@
             pltpu.VMEM((128, 1024), F32),
             pltpu.VMEM((512, 128), F32),
             pltpu.VMEM((64, 128), F32),
+            pltpu.VMEM((1, 128), F32),
+            pltpu.VMEM((1, 128), F32),
+            pltpu.VMEM((1, 128), F32),
             pltpu.VMEM((512, 384), BF),
             pltpu.VMEM((128, 384), BF),
             pltpu.VMEM((128, 384), BF),
@@ -485,7 +500,7 @@
             pltpu.SemaphoreType.DMA((PHASES,)),
             pltpu.SemaphoreType.DMA((PHASES,)),
             pltpu.SemaphoreType.REGULAR((NZ,)),
-            pltpu.SemaphoreType.DMA((7,)),
+            pltpu.SemaphoreType.DMA((12,)),
         ],
         compiler_params=pltpu.CompilerParams(
             collective_id=0, has_side_effects=True, vmem_limit_bytes=56 * 1024 * 1024

time: 101 us -> 100 us (0.990)
  no operation moved by 1% of the time
where the time goes in v3:
time: 100 us; the launch traced here: 99.9 us
  Pallas kernels  99.9 us (100%)
    pallas_call x1, Pallas kernels, shards(): pl.pallas_call(kernel, out_shape=(jax.ShapeDtypeStruct((4, 8, 2, 16, 128)...  97.6 us
    pallas_call x1, Pallas kernels, shards(): pl.pallas_call(add_mirrored, grid=(2,), out_shape=jax.ShapeDtypeStruct((6...  2.33 us

profile of v3, /device:TPU:24, one launch (start us, length us, event | category | flops | bytes accessed | tf_op | source)
XLA Modules:
  0.0 99.9 jit_solution(2500844012291940657)
XLA Ops:
  0.0 97.6 %triangle.1 = (f32[4,8,2,16,128]{4,3,2,1,0:T(8,128)}, f32[4,8,32,128]{3,2,1,0:T(8,128)}) custom-call(f32[2,4,8,32,128]{4,3,2,1,0:T(8,128)} %bitcast.7, f32[1,128]{1,0:T(1,128)} %bitcast.9, f32[128,512]{1,0:T(8,128)} %w_in_hbm.1, f32[128,128]{1,0:T(8,128)} %w_gate_hbm.1, f32[128,128]{1,0:T(8,128)} %w_out_hbm.1, f32[1,128]{1,0:T(1,128)} %bitcast.10, ...), custom_call_target="tpu_custom_call" | custom-call | tf_op jit(solution)/shard_map/triangle/pallas_call | solution.py:462
  97.6 2.3 %add_mirrored.1 = f32[64,32,64]{2,1,0:T(8,128)} custom-call(f32[4,8,2,16,128]{4,3,2,1,0:T(8,128)} %get-tuple-element.7.a1, f32[4,8,32,128]{3,2,1,0:T(8,128)} %get-tuple-element.8.a2f, f32[1,64]{1,0:T(1,128)} %bitcast.12), custom_call_target="tpu_custom_call" | custom-call | tf_op jit(solution)/shard_map/add_mirrored/pallas_call | solution.py:521

commit v4 on v3

--- a/solution.py
+++ b/solution.py
@@ -380,7 +380,7 @@
                 at = part * 256
                 up_gate = dot(wti3[at : at + 256, :], right)
                 up = dot(wti3[512 + at : 768 + at, :], right)
-                high, low = split(up_gate * sigmoid(up_gate) * up)
+                high, low = split(up_gate / (1.0 + jnp.exp(-up_gate)) * up)
                 total = total + dot(wto3[:, at : at + 256], high)
                 total = total + dot(wto3[:, 512 + at : 768 + at], low)
                 total = total + dot(wto3[:, 1024 + at : 1280 + at], high)
@@ -389,6 +389,8 @@
             for u in range(2):
                 abuf[hb, u * 128 : (u + 1) * 128, :] = stacked[:, u * 128 : (u + 1) * 128].T
         mirror(hb)
+
+    def own_logits(hb):
         to_plane(
             A1 + hb,
             lambda qq: abuf.at[hb, pl.ds(pl.multiple_of(qq * 16, 16), 16), :],
@@ -414,10 +416,14 @@
 
     landed(PROD, prb.at[0])
     transition(0, 0)
+    own_logits(0)
     transition(0, 1)
+    own_logits(1)
     landed(PROD + 1, prb.at[1])
     transition(1, 0)
     transition(1, 1)
+    own_logits(2)
+    own_logits(3)
 
     for hb in range(4):
         landed(A1 + hb, a1.at[hb])

time: 100 us -> 99.8 us (level)
  no operation moved by 1% of the time
where the time goes in v4:
time: 99.8 us; the launch traced here: 99.7 us
  Pallas kernels  99.6 us (100%)
    pallas_call x1, Pallas kernels, shards(): pl.pallas_call(kernel, out_shape=(jax.ShapeDtypeStruct((4, 8, 2, 16, 128)...  97.3 us
    pallas_call x1, Pallas kernels, shards(): pl.pallas_call(add_mirrored, grid=(2,), out_shape=jax.ShapeDtypeStruct((6...  2.33 us

profile of v4, /device:TPU:24, one launch (start us, length us, event | category | flops | bytes accessed | tf_op | source)
XLA Modules:
  0.0 99.7 jit_solution(5805769326210915086)
XLA Ops:
  0.0 97.3 %triangle.1 = (f32[4,8,2,16,128]{4,3,2,1,0:T(8,128)}, f32[4,8,32,128]{3,2,1,0:T(8,128)}) custom-call(f32[2,4,8,32,128]{4,3,2,1,0:T(8,128)} %bitcast.7, f32[1,128]{1,0:T(1,128)} %bitcast.9, f32[128,512]{1,0:T(8,128)} %w_in_hbm.1, f32[128,128]{1,0:T(8,128)} %w_gate_hbm.1, f32[128,128]{1,0:T(8,128)} %w_out_hbm.1, f32[1,128]{1,0:T(1,128)} %bitcast.10, ...), custom_call_target="tpu_custom_call" | custom-call | tf_op jit(solution)/shard_map/triangle/pallas_call | solution.py:468
  97.3 2.3 %add_mirrored.1 = f32[64,32,64]{2,1,0:T(8,128)} custom-call(f32[4,8,2,16,128]{4,3,2,1,0:T(8,128)} %get-tuple-element.7.a1, f32[4,8,32,128]{3,2,1,0:T(8,128)} %get-tuple-element.8.a2f, f32[1,64]{1,0:T(1,128)} %bitcast.12), custom_call_target="tpu_custom_call" | custom-call | tf_op jit(solution)/shard_map/add_mirrored/pallas_call | solution.py:527
